TPU v7x, 32 devices: a whole 2x2x4 slice. The times are simulated.
32 devices in a mesh: grp: 2 (over x), ex: 16 (over z, y, core).
Axes of the slice: x: 2, y: 2, z: 4, core: 2. Of those that a mesh axis runs over, the one named last changes fastest.
Arguments:
- query_factors: bfloat16 [1, 2, 4096, 128], P(None, None, None, 'ex'), may hold values from -6 to 6
- eigen_basis: bfloat16 [1, 2, 4096, 4096], P(None, None, None, 'ex'), may hold values from -0.09375 to 0.09375
- eigen_values: float32 [1, 2, 4096], P(None, None, 'ex'), may hold values from 0.05 to 20
- train_factors: bfloat16 [1, 2, 4096, 16384], P(None, None, None, ('grp', 'ex')), parts along dimension 3, may hold values from -0.046875 to 0.046875
Outputs:
- scores: float32 [16, 512], P(None, ('grp', 'ex')), parts along dimension 1
There are 2 independent parts, one for each index of `grp`. A program takes and returns all parts, laid end to end along the dimension named above; an argument that names none is the same for every part. Nothing has to cross between parts.
All inputs are finite; a program needn't handle non-finite values.
Results may differ from a plain program's by a relative error of at most 0.004.
Values may be sent and summed in bfloat16 or wider, within the bound.
A program may use at most 64 MiB of HBM per device.

v0:
```python
import math

import jax
import jax.numpy as jnp
from jax import lax
from jax.sharding import PartitionSpec as P

LAYERS = 1
RANK = 32
QRANK = 8


damping_term = 0.1


def passed_along(value, axis, steps):
    count = lax.axis_size(axis)
    pairs = [(source, (source + steps) % count) for source in range(count)]
    return lax.ppermute(value, axis, pairs)


def combine_grams(grams):
    joined = jnp.sum(grams[:, 0] * grams[:, 1], axis=0)
    count_q = joined.shape[0] // QRANK
    count_t = joined.shape[1] // RANK
    joined = joined.reshape(count_q, QRANK, count_t, RANK)
    return jnp.sum(joined, axis=(1, 3))


def partial_gram(piece, train_factors, start):
    rows = lax.dynamic_slice_in_dim(train_factors, start, piece.shape[2], 2)
    return jnp.einsum("lsdc,lsdt->lsct", piece, rows, preferred_element_type=jnp.float32)


def per_device(query_factors, eigen_basis, eigen_values, train_factors):
    gathered = lax.all_gather(query_factors, "ex", axis=3, tiled=True)
    product = jnp.einsum(
        "lski,lskc->lsic", eigen_basis, gathered, preferred_element_type=jnp.float32
    )
    scale = 1.0 / (eigen_values + damping_term)
    rotated = (product * scale[..., None]).astype(jnp.bfloat16)
    normalize = 1.0 / math.sqrt(LAYERS * QRANK * RANK)
    start_carry = jnp.zeros(
        (rotated.shape[0], 2, rotated.shape[3], train_factors.shape[3]), jnp.float32
    )
    count = lax.axis_size("ex")
    mine = lax.axis_index("ex")
    height = rotated.shape[2]

    def add_block(block, grams, turn):
        anchor = (mine - turn) % count * height
        return grams + partial_gram(block, train_factors, anchor)

    def advance(turn, state):
        block, grams = state
        grams = add_block(block, grams, turn)
        block = passed_along(block, "ex", 1)
        return (block, grams)

    block, grams = lax.fori_loop(0, count - 1, advance, (rotated, start_carry))
    grams = add_block(block, grams, jnp.int32(count - 1))
    scores = combine_grams(grams)
    return scores * normalize


def solution(mesh):
    in_specs = (
        P(None, None, None, "ex"),
        P(None, None, None, "ex"),
        P(None, None, "ex"),
        P(None, None, None, ("grp", "ex")),
    )
    out_specs = P(None, ("grp", "ex"))
    return jax.shard_map(
        per_device, mesh=mesh, in_specs=in_specs, out_specs=out_specs, check_vma=False
    )
```

profile of v0, /device:TPU:0, one launch (start us, length us, event | category | flops | bytes accessed | tf_op | source)
XLA Modules:
  0.0 179.3 jit_solution(13082386519024267280)
XLA Ops:
  6.5 1.7 copy.10
  9.0 44.7 %all-gather.2.cloned.1.call-done = bf16[1,2,4096,128]{2,1,0,3:T(2,128)(2,1)} async-done(((bf16[1,2,4096,8]{2,1,0,3:T(2,128)(2,1)}), bf16[1,2,4096,128]{2,1,0,3:T(2,128)(2,1)}) %all-gather.2.cloned.1.call-update) | async-done | bytes 2097168 | tf_op jit(solution)/shard_map/all_gather | solution.py:36
  53.7 4.9 %copy.11 = bf16[1,2,4096,128]{3,2,1,0:T(8,128)(2,1)S(1)} copy(bf16[1,2,4096,128]{2,1,0,3:T(2,128)(2,1)} %all-gather.2.cloned.1.call-done) | data formatting | bytes 4194304 | tf_op jit(solution)/shard_map/all_gather | solution.py:36
  58.5 4.0 %fusion.19 = bf16[1,2,256,128]{3,2,1,0:T(8,128)(2,1)S(1)} fusion(bf16[1,2,4096,128]{3,2,1,0:T(8,128)(2,1)S(1)} %copy.11, bf16[1,2,4096,256]{3,2,1,0:T(8,128)(2,1)} %param.7, f32[2,256]{1,0:T(2,128)S(1)} %divide_bitcast_fusion), kind=kOutput, calls=%fused_computation.13 | convolution fusion | flops 537001984 | bytes 6424576 | tf_op jit(solution)/shard_map/lski,lskc->lsic/dot_general | solution.py:37
  62.5 107.4 %while.18 = (s32[]{:T(128)}, bf16[1,2,256,128]{3,2,1,0:T(8,128)(2,1)S(1)}, f32[1,2,128,512]{2,3,1,0:T(8,128)S(1)}, s32[]{:T(128)}, bf16[1,2,4096,512]{3,2,1,0:T(...) while((s32[]{:T(128)}, ...), condition=%wide.region_1.2_spmd.clone, body=%wide.region_0.1_spmd.clone.sunk | while | flops 67371024 | bytes 2490698 | solution.py:60
  64.3 5.4 %collective-permute-done = bf16[1,2,256,128]{3,2,1,0:T(8,128)(2,1)S(1)} collective-permute-done((bf16[1,2,256,128]{3,2,1,0:T(8,128)(2,1)S(1)}, bf16[1,2,256,128]{3,2,1,0:T(8,128)(2,1)S(1)}, u32[]{:S(2)}, u32[]{:S(2)}) %collective-permute-start) | collective-permute-done | bytes 131104 | tf_op jit(solution)/shard_map/while/body/eval_jaxpr/ppermute | solution.py:19
  71.3 5.6 %collective-permute-done = bf16[1,2,256,128]{3,2,1,0:T(8,128)(2,1)S(1)} collective-permute-done((bf16[1,2,256,128]{3,2,1,0:T(8,128)(2,1)S(1)}, bf16[1,2,256,128]{3,2,1,0:T(8,128)(2,1)S(1)}, u32[]{:S(2)}, u32[]{:S(2)}) %collective-permute-start) | collective-permute-done | bytes 131104 | tf_op jit(solution)/shard_map/while/body/eval_jaxpr/ppermute | solution.py:19
  78.4 5.6 %collective-permute-done = bf16[1,2,256,128]{3,2,1,0:T(8,128)(2,1)S(1)} collective-permute-done((bf16[1,2,256,128]{3,2,1,0:T(8,128)(2,1)S(1)}, bf16[1,2,256,128]{3,2,1,0:T(8,128)(2,1)S(1)}, u32[]{:S(2)}, u32[]{:S(2)}) %collective-permute-start) | collective-permute-done | bytes 131104 | tf_op jit(solution)/shard_map/while/body/eval_jaxpr/ppermute | solution.py:19
  84.1 1.5 fusion.33
  85.6 5.6 %collective-permute-done = bf16[1,2,256,128]{3,2,1,0:T(8,128)(2,1)S(1)} collective-permute-done((bf16[1,2,256,128]{3,2,1,0:T(8,128)(2,1)S(1)}, bf16[1,2,256,128]{3,2,1,0:T(8,128)(2,1)S(1)}, u32[]{:S(2)}, u32[]{:S(2)}) %collective-permute-start) | collective-permute-done | bytes 131104 | tf_op jit(solution)/shard_map/while/body/eval_jaxpr/ppermute | solution.py:19
  91.3 1.5 fusion.33
  92.7 5.6 %collective-permute-done = bf16[1,2,256,128]{3,2,1,0:T(8,128)(2,1)S(1)} collective-permute-done((bf16[1,2,256,128]{3,2,1,0:T(8,128)(2,1)S(1)}, bf16[1,2,256,128]{3,2,1,0:T(8,128)(2,1)S(1)}, u32[]{:S(2)}, u32[]{:S(2)}) %collective-permute-start) | collective-permute-done | bytes 131104 | tf_op jit(solution)/shard_map/while/body/eval_jaxpr/ppermute | solution.py:19
  99.9 5.6 %collective-permute-done = bf16[1,2,256,128]{3,2,1,0:T(8,128)(2,1)S(1)} collective-permute-done((bf16[1,2,256,128]{3,2,1,0:T(8,128)(2,1)S(1)}, bf16[1,2,256,128]{3,2,1,0:T(8,128)(2,1)S(1)}, u32[]{:S(2)}, u32[]{:S(2)}) %collective-permute-start) | collective-permute-done | bytes 131104 | tf_op jit(solution)/shard_map/while/body/eval_jaxpr/ppermute | solution.py:19
  107.0 5.6 %collective-permute-done = bf16[1,2,256,128]{3,2,1,0:T(8,128)(2,1)S(1)} collective-permute-done((bf16[1,2,256,128]{3,2,1,0:T(8,128)(2,1)S(1)}, bf16[1,2,256,128]{3,2,1,0:T(8,128)(2,1)S(1)}, u32[]{:S(2)}, u32[]{:S(2)}) %collective-permute-start) | collective-permute-done | bytes 131104 | tf_op jit(solution)/shard_map/while/body/eval_jaxpr/ppermute | solution.py:19
  114.2 5.6 %collective-permute-done = bf16[1,2,256,128]{3,2,1,0:T(8,128)(2,1)S(1)} collective-permute-done((bf16[1,2,256,128]{3,2,1,0:T(8,128)(2,1)S(1)}, bf16[1,2,256,128]{3,2,1,0:T(8,128)(2,1)S(1)}, u32[]{:S(2)}, u32[]{:S(2)}) %collective-permute-start) | collective-permute-done | bytes 131104 | tf_op jit(solution)/shard_map/while/body/eval_jaxpr/ppermute | solution.py:19
  119.9 1.5 fusion.33
  121.4 5.6 %collective-permute-done = bf16[1,2,256,128]{3,2,1,0:T(8,128)(2,1)S(1)} collective-permute-done((bf16[1,2,256,128]{3,2,1,0:T(8,128)(2,1)S(1)}, bf16[1,2,256,128]{3,2,1,0:T(8,128)(2,1)S(1)}, u32[]{:S(2)}, u32[]{:S(2)}) %collective-permute-start) | collective-permute-done | bytes 131104 | tf_op jit(solution)/shard_map/while/body/eval_jaxpr/ppermute | solution.py:19
  128.5 5.6 %collective-permute-done = bf16[1,2,256,128]{3,2,1,0:T(8,128)(2,1)S(1)} collective-permute-done((bf16[1,2,256,128]{3,2,1,0:T(8,128)(2,1)S(1)}, bf16[1,2,256,128]{3,2,1,0:T(8,128)(2,1)S(1)}, u32[]{:S(2)}, u32[]{:S(2)}) %collective-permute-start) | collective-permute-done | bytes 131104 | tf_op jit(solution)/shard_map/while/body/eval_jaxpr/ppermute | solution.py:19
  135.7 5.6 %collective-permute-done = bf16[1,2,256,128]{3,2,1,0:T(8,128)(2,1)S(1)} collective-permute-done((bf16[1,2,256,128]{3,2,1,0:T(8,128)(2,1)S(1)}, bf16[1,2,256,128]{3,2,1,0:T(8,128)(2,1)S(1)}, u32[]{:S(2)}, u32[]{:S(2)}) %collective-permute-start) | collective-permute-done | bytes 131104 | tf_op jit(solution)/shard_map/while/body/eval_jaxpr/ppermute | solution.py:19
  142.8 5.6 %collective-permute-done = bf16[1,2,256,128]{3,2,1,0:T(8,128)(2,1)S(1)} collective-permute-done((bf16[1,2,256,128]{3,2,1,0:T(8,128)(2,1)S(1)}, bf16[1,2,256,128]{3,2,1,0:T(8,128)(2,1)S(1)}, u32[]{:S(2)}, u32[]{:S(2)}) %collective-permute-start) | collective-permute-done | bytes 131104 | tf_op jit(solution)/shard_map/while/body/eval_jaxpr/ppermute | solution.py:19
  148.5 1.5 fusion.33
  150.0 5.6 %collective-permute-done = bf16[1,2,256,128]{3,2,1,0:T(8,128)(2,1)S(1)} collective-permute-done((bf16[1,2,256,128]{3,2,1,0:T(8,128)(2,1)S(1)}, bf16[1,2,256,128]{3,2,1,0:T(8,128)(2,1)S(1)}, u32[]{:S(2)}, u32[]{:S(2)}) %collective-permute-start) | collective-permute-done | bytes 131104 | tf_op jit(solution)/shard_map/while/body/eval_jaxpr/ppermute | solution.py:19
  157.1 5.6 %collective-permute-done = bf16[1,2,256,128]{3,2,1,0:T(8,128)(2,1)S(1)} collective-permute-done((bf16[1,2,256,128]{3,2,1,0:T(8,128)(2,1)S(1)}, bf16[1,2,256,128]{3,2,1,0:T(8,128)(2,1)S(1)}, u32[]{:S(2)}, u32[]{:S(2)}) %collective-permute-start) | collective-permute-done | bytes 131104 | tf_op jit(solution)/shard_map/while/body/eval_jaxpr/ppermute | solution.py:19
  164.3 5.6 %collective-permute-done = bf16[1,2,256,128]{3,2,1,0:T(8,128)(2,1)S(1)} collective-permute-done((bf16[1,2,256,128]{3,2,1,0:T(8,128)(2,1)S(1)}, bf16[1,2,256,128]{3,2,1,0:T(8,128)(2,1)S(1)}, u32[]{:S(2)}, u32[]{:S(2)}) %collective-permute-start) | collective-permute-done | bytes 131104 | tf_op jit(solution)/shard_map/while/body/eval_jaxpr/ppermute | solution.py:19
  (51 shorter events, 20.6 us)
Async XLA Ops:
  6.5 47.1 %all-gather.2.cloned.1.call-start = ((), (), s32[]{:S(2)}) async-start(), calls=%async_computation | async-start | bytes 2228224 | tf_op jit(solution)/shard_map/all_gather | solution.py:36
  62.5 7.1 %collective-permute-start = (bf16[1,2,256,128]{3,2,1,0:T(8,128)(2,1)S(1)}, bf16[1,2,256,128]{3,2,1,0:T(8,128)(2,1)S(1)}, u32[]{:S(2)}, u32[]{:S(2)}) collective-permute-start(bf16[1,2,256,128]{3,2,1,0:T(8,128)(2,1)S(1)} %copy.23), channel_id=1, source_target_pairs={{0,1},{1,2},{2,3},{3,4},{4,5},{5,6},{6,7},{7,8},{8,9},{9,10},{10,1... | collective-permute-start | bytes 393224 | tf_op jit(solution)/shard_map/while/body/eval_jaxpr/ppermute | solution.py:19
  69.7 7.1 %collective-permute-start = (bf16[1,2,256,128]{3,2,1,0:T(8,128)(2,1)S(1)}, bf16[1,2,256,128]{3,2,1,0:T(8,128)(2,1)S(1)}, u32[]{:S(2)}, u32[]{:S(2)}) collective-permute-start(bf16[1,2,256,128]{3,2,1,0:T(8,128)(2,1)S(1)} %copy.23), channel_id=1, source_target_pairs={{0,1},{1,2},{2,3},{3,4},{4,5},{5,6},{6,7},{7,8},{8,9},{9,10},{10,1... | collective-permute-start | bytes 393224 | tf_op jit(solution)/shard_map/while/body/eval_jaxpr/ppermute | solution.py:19
  76.8 7.1 %collective-permute-start = (bf16[1,2,256,128]{3,2,1,0:T(8,128)(2,1)S(1)}, bf16[1,2,256,128]{3,2,1,0:T(8,128)(2,1)S(1)}, u32[]{:S(2)}, u32[]{:S(2)}) collective-permute-start(bf16[1,2,256,128]{3,2,1,0:T(8,128)(2,1)S(1)} %copy.23), channel_id=1, source_target_pairs={{0,1},{1,2},{2,3},{3,4},{4,5},{5,6},{6,7},{7,8},{8,9},{9,10},{10,1... | collective-permute-start | bytes 393224 | tf_op jit(solution)/shard_map/while/body/eval_jaxpr/ppermute | solution.py:19
  84.0 7.1 %collective-permute-start = (bf16[1,2,256,128]{3,2,1,0:T(8,128)(2,1)S(1)}, bf16[1,2,256,128]{3,2,1,0:T(8,128)(2,1)S(1)}, u32[]{:S(2)}, u32[]{:S(2)}) collective-permute-start(bf16[1,2,256,128]{3,2,1,0:T(8,128)(2,1)S(1)} %copy.23), channel_id=1, source_target_pairs={{0,1},{1,2},{2,3},{3,4},{4,5},{5,6},{6,7},{7,8},{8,9},{9,10},{10,1... | collective-permute-start | bytes 393224 | tf_op jit(solution)/shard_map/while/body/eval_jaxpr/ppermute | solution.py:19
  91.2 7.1 %collective-permute-start = (bf16[1,2,256,128]{3,2,1,0:T(8,128)(2,1)S(1)}, bf16[1,2,256,128]{3,2,1,0:T(8,128)(2,1)S(1)}, u32[]{:S(2)}, u32[]{:S(2)}) collective-permute-start(bf16[1,2,256,128]{3,2,1,0:T(8,128)(2,1)S(1)} %copy.23), channel_id=1, source_target_pairs={{0,1},{1,2},{2,3},{3,4},{4,5},{5,6},{6,7},{7,8},{8,9},{9,10},{10,1... | collective-permute-start | bytes 393224 | tf_op jit(solution)/shard_map/while/body/eval_jaxpr/ppermute | solution.py:19
  98.3 7.1 %collective-permute-start = (bf16[1,2,256,128]{3,2,1,0:T(8,128)(2,1)S(1)}, bf16[1,2,256,128]{3,2,1,0:T(8,128)(2,1)S(1)}, u32[]{:S(2)}, u32[]{:S(2)}) collective-permute-start(bf16[1,2,256,128]{3,2,1,0:T(8,128)(2,1)S(1)} %copy.23), channel_id=1, source_target_pairs={{0,1},{1,2},{2,3},{3,4},{4,5},{5,6},{6,7},{7,8},{8,9},{9,10},{10,1... | collective-permute-start | bytes 393224 | tf_op jit(solution)/shard_map/while/body/eval_jaxpr/ppermute | solution.py:19
  105.5 7.1 %collective-permute-start = (bf16[1,2,256,128]{3,2,1,0:T(8,128)(2,1)S(1)}, bf16[1,2,256,128]{3,2,1,0:T(8,128)(2,1)S(1)}, u32[]{:S(2)}, u32[]{:S(2)}) collective-permute-start(bf16[1,2,256,128]{3,2,1,0:T(8,128)(2,1)S(1)} %copy.23), channel_id=1, source_target_pairs={{0,1},{1,2},{2,3},{3,4},{4,5},{5,6},{6,7},{7,8},{8,9},{9,10},{10,1... | collective-permute-start | bytes 393224 | tf_op jit(solution)/shard_map/while/body/eval_jaxpr/ppermute | solution.py:19
  112.6 7.1 %collective-permute-start = (bf16[1,2,256,128]{3,2,1,0:T(8,128)(2,1)S(1)}, bf16[1,2,256,128]{3,2,1,0:T(8,128)(2,1)S(1)}, u32[]{:S(2)}, u32[]{:S(2)}) collective-permute-start(bf16[1,2,256,128]{3,2,1,0:T(8,128)(2,1)S(1)} %copy.23), channel_id=1, source_target_pairs={{0,1},{1,2},{2,3},{3,4},{4,5},{5,6},{6,7},{7,8},{8,9},{9,10},{10,1... | collective-permute-start | bytes 393224 | tf_op jit(solution)/shard_map/while/body/eval_jaxpr/ppermute | solution.py:19
  119.8 7.1 %collective-permute-start = (bf16[1,2,256,128]{3,2,1,0:T(8,128)(2,1)S(1)}, bf16[1,2,256,128]{3,2,1,0:T(8,128)(2,1)S(1)}, u32[]{:S(2)}, u32[]{:S(2)}) collective-permute-start(bf16[1,2,256,128]{3,2,1,0:T(8,128)(2,1)S(1)} %copy.23), channel_id=1, source_target_pairs={{0,1},{1,2},{2,3},{3,4},{4,5},{5,6},{6,7},{7,8},{8,9},{9,10},{10,1... | collective-permute-start | bytes 393224 | tf_op jit(solution)/shard_map/while/body/eval_jaxpr/ppermute | solution.py:19
  126.9 7.1 %collective-permute-start = (bf16[1,2,256,128]{3,2,1,0:T(8,128)(2,1)S(1)}, bf16[1,2,256,128]{3,2,1,0:T(8,128)(2,1)S(1)}, u32[]{:S(2)}, u32[]{:S(2)}) collective-permute-start(bf16[1,2,256,128]{3,2,1,0:T(8,128)(2,1)S(1)} %copy.23), channel_id=1, source_target_pairs={{0,1},{1,2},{2,3},{3,4},{4,5},{5,6},{6,7},{7,8},{8,9},{9,10},{10,1... | collective-permute-start | bytes 393224 | tf_op jit(solution)/shard_map/while/body/eval_jaxpr/ppermute | solution.py:19
  134.1 7.1 %collective-permute-start = (bf16[1,2,256,128]{3,2,1,0:T(8,128)(2,1)S(1)}, bf16[1,2,256,128]{3,2,1,0:T(8,128)(2,1)S(1)}, u32[]{:S(2)}, u32[]{:S(2)}) collective-permute-start(bf16[1,2,256,128]{3,2,1,0:T(8,128)(2,1)S(1)} %copy.23), channel_id=1, source_target_pairs={{0,1},{1,2},{2,3},{3,4},{4,5},{5,6},{6,7},{7,8},{8,9},{9,10},{10,1... | collective-permute-start | bytes 393224 | tf_op jit(solution)/shard_map/while/body/eval_jaxpr/ppermute | solution.py:19
  141.3 7.1 %collective-permute-start = (bf16[1,2,256,128]{3,2,1,0:T(8,128)(2,1)S(1)}, bf16[1,2,256,128]{3,2,1,0:T(8,128)(2,1)S(1)}, u32[]{:S(2)}, u32[]{:S(2)}) collective-permute-start(bf16[1,2,256,128]{3,2,1,0:T(8,128)(2,1)S(1)} %copy.23), channel_id=1, source_target_pairs={{0,1},{1,2},{2,3},{3,4},{4,5},{5,6},{6,7},{7,8},{8,9},{9,10},{10,1... | collective-permute-start | bytes 393224 | tf_op jit(solution)/shard_map/while/body/eval_jaxpr/ppermute | solution.py:19
  148.4 7.1 %collective-permute-start = (bf16[1,2,256,128]{3,2,1,0:T(8,128)(2,1)S(1)}, bf16[1,2,256,128]{3,2,1,0:T(8,128)(2,1)S(1)}, u32[]{:S(2)}, u32[]{:S(2)}) collective-permute-start(bf16[1,2,256,128]{3,2,1,0:T(8,128)(2,1)S(1)} %copy.23), channel_id=1, source_target_pairs={{0,1},{1,2},{2,3},{3,4},{4,5},{5,6},{6,7},{7,8},{8,9},{9,10},{10,1... | collective-permute-start | bytes 393224 | tf_op jit(solution)/shard_map/while/body/eval_jaxpr/ppermute | solution.py:19
  155.6 7.1 %collective-permute-start = (bf16[1,2,256,128]{3,2,1,0:T(8,128)(2,1)S(1)}, bf16[1,2,256,128]{3,2,1,0:T(8,128)(2,1)S(1)}, u32[]{:S(2)}, u32[]{:S(2)}) collective-permute-start(bf16[1,2,256,128]{3,2,1,0:T(8,128)(2,1)S(1)} %copy.23), channel_id=1, source_target_pairs={{0,1},{1,2},{2,3},{3,4},{4,5},{5,6},{6,7},{7,8},{8,9},{9,10},{10,1... | collective-permute-start | bytes 393224 | tf_op jit(solution)/shard_map/while/body/eval_jaxpr/ppermute | solution.py:19
  162.7 7.1 %collective-permute-start = (bf16[1,2,256,128]{3,2,1,0:T(8,128)(2,1)S(1)}, bf16[1,2,256,128]{3,2,1,0:T(8,128)(2,1)S(1)}, u32[]{:S(2)}, u32[]{:S(2)}) collective-permute-start(bf16[1,2,256,128]{3,2,1,0:T(8,128)(2,1)S(1)} %copy.23), channel_id=1, source_target_pairs={{0,1},{1,2},{2,3},{3,4},{4,5},{5,6},{6,7},{7,8},{8,9},{9,10},{10,1... | collective-permute-start | bytes 393224 | tf_op jit(solution)/shard_map/while/body/eval_jaxpr/ppermute | solution.py:19
Sparse Core Ops, SparseCore 0:
  9.5 44.0 all-gather.1
where the time goes:
time: 180 us; the launch traced here: 179 us
  waiting for transfers between devices  128 us (71%)
  matrix products  27.2 us (15%)
  between operations  13.5 us (8%)
  local copies, waits for them, and re-layouts  7.2 us (4%)
    ppermute x15, waiting for transfers between devices, passed_along(): return lax.ppermute(value, axis, pairs)  83.4 us
    all_gather x1, waiting for transfers between devices, per_device(): gathered = lax.all_gather(query_factors, 'ex', axis=3, tiled=True)  44.7 us
    dot_general x16, matrix products, partial_gram(): jnp.einsum('lsdc,lsdt->lsct', piece, rows, preferred_element_type=jnp.flo...  23.3 us
    all_gather x1, local copies, waits for them, and re-layouts, per_device(): gathered = lax.all_gather(query_factors, 'ex', axis=3, tiled=True)  4.88 us
    dot_general x1, matrix products, per_device(): jnp.einsum('lski,lskc->lsic', eigen_basis, gathered, preferred_element_ty...  3.96 us
  transfers between devices with their start and end apart: 16, of which 16 were waited for; matrix products, arithmetic and copies ran while one was open for 13% of the time, Pallas kernels for 0%

commit v1 on v0

v1 whole, which is shorter than its diff:
```python
import functools
import math

import jax
import jax.numpy as jnp
from jax import lax
from jax.experimental import pallas as pl
from jax.experimental.pallas import tpu as pltpu
from jax.sharding import PartitionSpec as P

LAYERS = 1
RANK = 32
QRANK = 8
DAMPING = 0.1
MESH = pl.DeviceIdType.MESH


def flipped(a, bits, count):
    step = 1
    while step < count:
        if bits & step:
            a = a + step - 2 * step * ((a // step) % 2)
        step *= 2
    return a


def kernel(
    nz, q_hbm, basis_hbm, values_ref, train_hbm, out_ref,
    q_in, q_all, basis, train, rot_all, gram, local_sem,
    q_recv, q_send_z, q_send_y, q_send_c,
    r_recv, r_send_z, r_send_y, r_send_x, r_send_c,
):
    grp = lax.axis_index("grp")
    mine = lax.axis_index("ex")
    core = mine % 2
    y = (mine // 2) % 2
    z = mine // 4
    side = grp % 2
    other = 1 - side
    partner = grp + 1 - 2 * side
    n = 4 * nz

    def at(zz, yy, cc):
        return (zz * 2 + yy) * 2 + cc

    zs = [flipped(z, j, nz) for j in range(nz)]
    z_dev = [(grp, at(zs[j], y, core)) for j in range(nz)]
    y_dev = (grp, at(z, 1 - y, core))
    c_dev = (grp, at(z, y, 1 - core))
    x_dev = (partner, mine)

    q_copy = pltpu.make_async_copy(q_hbm.at[side], q_in, local_sem.at[0])
    q_copy.start()
    basis_copy = pltpu.make_async_copy(basis_hbm.at[0, side], basis, local_sem.at[1])
    basis_copy.start()
    train_copy = pltpu.make_async_copy(train_hbm.at[0], train, local_sem.at[2])
    train_copy.start()

    barrier = pltpu.get_barrier_semaphore()
    partners = z_dev[1:] + [y_dev, c_dev, x_dev]
    for device in partners:
        pl.semaphore_signal(barrier, inc=1, device_id=device, device_id_type=MESH)

    q_copy.wait()
    half = q_in.shape[1] // 2
    whole = q_in[...].astype(jnp.float32)
    stacked = jnp.concatenate([whole[:, :half], whole[:, half:]], axis=0)
    q_all[mine] = stacked.astype(q_all.dtype)

    pl.semaphore_wait(barrier, len(partners))

    started = []

    def send(slot, send_sem, recv_sem, device):
        copy = pltpu.make_async_remote_copy(
            src_ref=slot, dst_ref=slot, send_sem=send_sem, recv_sem=recv_sem,
            device_id=device, device_id_type=MESH,
        )
        copy.start()
        started.append(copy)

    def arrived(slot, recv_sem, device):
        pltpu.make_async_remote_copy(
            src_ref=slot, dst_ref=slot, send_sem=local_sem.at[0], recv_sem=recv_sem,
            device_id=device, device_id_type=MESH,
        ).wait_recv()

    def q_send(e, send_sem, device):
        send(q_all.at[e], send_sem, q_recv.at[e], device)

    def q_arrived(e, device):
        arrived(q_all.at[e], q_recv.at[e], device)

    for j in range(1, nz):
        q_send(mine, q_send_z.at[j], z_dev[j])
    for j in range(nz):
        e = at(zs[j], y, core)
        if j:
            q_arrived(e, z_dev[j])
        q_send(e, q_send_y.at[j], y_dev)
        q_send(e, q_send_c.at[j], c_dev)
    for j in range(nz):
        e = at(zs[j], 1 - y, core)
        q_arrived(e, y_dev)
        q_send(e, q_send_c.at[nz + j], c_dev)
    for yy in range(2):
        for j in range(nz):
            q_arrived(at(zs[j], flipped(y, yy, 2), 1 - core), c_dev)

    basis_copy.wait()
    width = basis.shape[1]
    rows = q_all[...].reshape(n * 16, half)
    low = jnp.dot(rows, basis[:half], preferred_element_type=jnp.float32)
    high = jnp.dot(rows, basis[half:], preferred_element_type=jnp.float32)
    product = low.reshape(n, 2, 8, width)[:, 0] + high.reshape(n, 2, 8, width)[:, 1]
    scale = 1.0 / (values_ref[pl.ds(side, 1), :] + DAMPING)
    rotated = product.reshape(n * 8, width) * scale
    rot_all[side, mine] = rotated.astype(rot_all.dtype)

    def r_send(s, e, send_sem, device):
        send(rot_all.at[s, e], send_sem, r_recv.at[s, e], device)

    def r_arrived(s, e, device):
        arrived(rot_all.at[s, e], r_recv.at[s, e], device)

    def add(s, e):
        rows = train[s, pl.ds(pl.multiple_of(e * width, width), width), :]
        gram[s] += jnp.dot(rot_all[s, e], rows, preferred_element_type=jnp.float32)

    cut = nz // 2
    for j in range(1, nz):
        r_send(side, mine, r_send_z.at[j], z_dev[j])
    gram[...] = jnp.zeros_like(gram)
    train_copy.wait()
    for j in range(nz):
        e = at(zs[j], y, core)
        if j:
            r_arrived(side, e, z_dev[j])
        r_send(side, e, r_send_x.at[j], x_dev)
        r_send(side, e, r_send_y.at[j], y_dev)
        r_send(side, e, r_send_c.at[j], c_dev)
        add(side, e)
    for j in range(nz):
        e = at(zs[j], y, core)
        r_arrived(other, e, x_dev)
        if j >= cut:
            r_send(other, e, r_send_y.at[nz + j], y_dev)
        r_send(other, e, r_send_c.at[nz + j], c_dev)
        add(other, e)
        e = at(zs[j], 1 - y, core)
        r_arrived(side, e, y_dev)
        if j < cut:
            r_send(side, e, r_send_x.at[nz + j], x_dev)
        r_send(side, e, r_send_c.at[2 * nz + j], c_dev)
        add(side, e)
    for j in range(nz):
        e = at(zs[j], 1 - y, core)
        r_arrived(other, e, x_dev if j < cut else y_dev)
        r_send(other, e, r_send_c.at[3 * nz + j], c_dev)
        add(other, e)
    for s, yy in ((side, y), (other, y), (side, 1 - y), (other, 1 - y)):
        for j in range(nz):
            e = at(zs[j], yy, 1 - core)
            r_arrived(s, e, c_dev)
            add(s, e)

    joined = gram[0] * gram[1]
    columns = joined.shape[1]
    by_query = jnp.sum(joined.reshape(joined.shape[0] // QRANK, QRANK, columns), axis=1)
    count_t = columns // RANK
    member = lax.broadcasted_iota(jnp.int32, (columns, count_t), 0) // RANK
    picks = member == lax.broadcasted_iota(jnp.int32, (columns, count_t), 1)
    scores = jnp.dot(
        by_query, picks.astype(jnp.float32), precision=lax.Precision.HIGHEST,
        preferred_element_type=jnp.float32,
    )
    out_ref[...] = scores * (1.0 / math.sqrt(LAYERS * QRANK * RANK))

    for copy in started:
        copy.wait_send()


def per_device(query_factors, eigen_basis, eigen_values, train_factors):
    n = lax.axis_size("ex")
    nz = n // 4
    depth, per = query_factors.shape[2:]
    width = eigen_basis.shape[3]
    tcols = train_factors.shape[3]
    queries = jnp.transpose(query_factors[0], (0, 2, 1))
    hbm = pl.BlockSpec(memory_space=pl.ANY)
    vmem = pl.BlockSpec(memory_space=pltpu.VMEM)
    dma = pltpu.SemaphoreType.DMA
    return pl.pallas_call(
        functools.partial(kernel, nz),
        out_shape=jax.ShapeDtypeStruct((n * per // QRANK, tcols // RANK), jnp.float32),
        in_specs=[hbm, hbm, vmem, hbm],
        out_specs=vmem,
        scratch_shapes=[
            pltpu.VMEM((per, depth), jnp.bfloat16),
            pltpu.VMEM((n, 2 * per, depth // 2), jnp.bfloat16),
            pltpu.VMEM((depth, width), jnp.bfloat16),
            pltpu.VMEM((2, depth, tcols), jnp.bfloat16),
            pltpu.VMEM((2, n, n * per, width), jnp.bfloat16),
            pltpu.VMEM((2, n * per, tcols), jnp.float32),
            dma((3,)),
            dma((n,)), dma((nz,)), dma((nz,)), dma((2 * nz,)),
            dma((2, n)), dma((nz,)), dma((2 * nz,)), dma((2 * nz,)), dma((4 * nz,)),
        ],
        compiler_params=pltpu.CompilerParams(
            collective_id=0, has_side_effects=True, vmem_limit_bytes=56 * 2**20
        ),
    )(queries, eigen_basis, eigen_values[0], train_factors)


def solution(mesh):
    in_specs = (
        P(None, None, None, "ex"),
        P(None, None, None, "ex"),
        P(None, None, "ex"),
        P(None, None, None, ("grp", "ex")),
    )
    out_specs = P(None, ("grp", "ex"))
    return jax.shard_map(
        per_device, mesh=mesh, in_specs=in_specs, out_specs=out_specs, check_vma=False
    )
```

time: 180 us -> 36.5 us (0.20)
  waiting for transfers between devices: 128 us -> 0 us
  Pallas kernels: 0 us -> 35 us
  matrix products: 27.2 us -> 0 us
  between operations: 13.5 us -> 0.01 us
  local copies, waits for them, and re-layouts: 7.2 us -> 1.3 us
    ppermute x15 -> x0, waiting for transfers between devices: 83.4 us -> none  [passed_along(): return lax.ppermute(value, axis, pairs)]
    all_gather x1 -> x0, waiting for transfers between devices: 44.7 us -> none  [per_device(): gathered = lax.all_gather(query_factors, 'ex', axis=3, tiled=True)]
    pallas_call x0 -> x1, Pallas kernels: none -> 35 us  [per_device(): pl.pallas_call(functools.partial(kernel, nz), out_shape=jax.ShapeDtypeStr...]
    dot_general x17 -> x0, matrix products: 27.2 us -> none  [the longest x16 23.3 us: partial_gram(): jnp.einsum('lsdc,lsdt->lsct', piece, rows, preferred_element_type=jnp.flo...]
    all_gather x1 -> x0, local copies, waits for them, and re-layouts: 4.88 us -> none  [per_device(): gathered = lax.all_gather(query_factors, 'ex', axis=3, tiled=True)]
  transfers between devices with their start and end apart: 16 -> 0, of which waited for: 16 -> 0; matrix products, arithmetic and copies ran while one was open for 13% -> 0% of each run, Pallas kernels for 0% -> 0%
where the time goes in v1:
time: 36.5 us; the launch traced here: 36.3 us
  Pallas kernels  35 us (96%)
  local copies, waits for them, and re-layouts  1.3 us (4%)
    pallas_call x1, Pallas kernels, per_device(): pl.pallas_call(functools.partial(kernel, nz), out_shape=jax.ShapeDtypeStr...  35 us
    unnamed x1, local copies, waits for them, and re-layouts  1.3 us

profile of v1, /device:TPU:0, one launch (start us, length us, event | category | flops | bytes accessed | tf_op | source)
XLA Modules:
  0.0 36.3 jit_solution(16703193257087557827)
XLA Ops:
  0.0 35.0 %shard_map.46 = f32[16,16]{1,0:T(8,128)} custom-call(bf16[2,8,4096]{2,1,0:T(8,128)(2,1)} %bitcast.4, bf16[1,2,4096,256]{3,2,1,0:T(8,128)(2,1)} %basis_hbm.1, f32[2,256]{1,0:T(2,128)} %bitcast.5, bf16[1,2,4096,512]{3,2,1,0:T(8,128)(2,1)} %train_hbm.1), custom_call_target="tpu_custom_call" | custom-call | tf_op jit(solution)/shard_map/pallas_call | solution.py:193
  35.0 1.3 %copy.6 = f32[16,16]{1,0:T(8,128)} copy(f32[16,16]{1,0:T(8,128)} %shard_map.46) | data formatting | bytes 2048

commit v2 on v1

--- a/solution.py
+++ b/solution.py
@@ -25,8 +25,8 @@
 
 
 def kernel(
-    nz, q_hbm, basis_hbm, values_ref, train_hbm, out_ref,
-    q_in, q_all, basis, train, rot_all, gram, local_sem,
+    nz, q_hbm, basis_hbm, values_hbm, train_hbm, out_ref,
+    values_ref, q_in, q_all, basis, train, rot_all, gram, local_sem,
     q_recv, q_send_z, q_send_y, q_send_c,
     r_recv, r_send_z, r_send_y, r_send_x, r_send_c,
 ):
@@ -49,17 +49,19 @@
     c_dev = (grp, at(z, y, 1 - core))
     x_dev = (partner, mine)
 
+    barrier = pltpu.get_barrier_semaphore()
+    partners = z_dev[1:] + [y_dev, c_dev, x_dev]
+    for device in partners:
+        pl.semaphore_signal(barrier, inc=1, device_id=device, device_id_type=MESH)
+
     q_copy = pltpu.make_async_copy(q_hbm.at[side], q_in, local_sem.at[0])
     q_copy.start()
     basis_copy = pltpu.make_async_copy(basis_hbm.at[0, side], basis, local_sem.at[1])
     basis_copy.start()
+    values_copy = pltpu.make_async_copy(values_hbm, values_ref, local_sem.at[3])
+    values_copy.start()
     train_copy = pltpu.make_async_copy(train_hbm.at[0], train, local_sem.at[2])
     train_copy.start()
-
-    barrier = pltpu.get_barrier_semaphore()
-    partners = z_dev[1:] + [y_dev, c_dev, x_dev]
-    for device in partners:
-        pl.semaphore_signal(barrier, inc=1, device_id=device, device_id_type=MESH)
 
     q_copy.wait()
     half = q_in.shape[1] // 2
@@ -108,6 +110,7 @@
             q_arrived(at(zs[j], flipped(y, yy, 2), 1 - core), c_dev)
 
     basis_copy.wait()
+    values_copy.wait()
     width = basis.shape[1]
     rows = q_all[...].reshape(n * 16, half)
     low = jnp.dot(rows, basis[:half], preferred_element_type=jnp.float32)
@@ -127,11 +130,8 @@
         rows = train[s, pl.ds(pl.multiple_of(e * width, width), width), :]
         gram[s] += jnp.dot(rot_all[s, e], rows, preferred_element_type=jnp.float32)
 
-    cut = nz // 2
     for j in range(1, nz):
         r_send(side, mine, r_send_z.at[j], z_dev[j])
-    gram[...] = jnp.zeros_like(gram)
-    train_copy.wait()
     for j in range(nz):
         e = at(zs[j], y, core)
         if j:
@@ -139,23 +139,26 @@
         r_send(side, e, r_send_x.at[j], x_dev)
         r_send(side, e, r_send_y.at[j], y_dev)
         r_send(side, e, r_send_c.at[j], c_dev)
+        if j == 0:
+            gram[...] = jnp.zeros_like(gram)
+            train_copy.wait()
         add(side, e)
     for j in range(nz):
         e = at(zs[j], y, core)
+        f = at(zs[j], 1 - y, core)
         r_arrived(other, e, x_dev)
-        if j >= cut:
+        if j % 2:
             r_send(other, e, r_send_y.at[nz + j], y_dev)
         r_send(other, e, r_send_c.at[nz + j], c_dev)
+        r_arrived(side, f, y_dev)
+        if j % 2 == 0:
+            r_send(side, f, r_send_x.at[nz + j], x_dev)
+        r_send(side, f, r_send_c.at[2 * nz + j], c_dev)
         add(other, e)
+        add(side, f)
+    for j in range(nz):
         e = at(zs[j], 1 - y, core)
-        r_arrived(side, e, y_dev)
-        if j < cut:
-            r_send(side, e, r_send_x.at[nz + j], x_dev)
-        r_send(side, e, r_send_c.at[2 * nz + j], c_dev)
-        add(side, e)
-    for j in range(nz):
-        e = at(zs[j], 1 - y, core)
-        r_arrived(other, e, x_dev if j < cut else y_dev)
+        r_arrived(other, e, y_dev if j % 2 else x_dev)
         r_send(other, e, r_send_c.at[3 * nz + j], c_dev)
         add(other, e)
     for s, yy in ((side, y), (other, y), (side, 1 - y), (other, 1 - y)):
@@ -193,16 +196,17 @@
     return pl.pallas_call(
         functools.partial(kernel, nz),
         out_shape=jax.ShapeDtypeStruct((n * per // QRANK, tcols // RANK), jnp.float32),
-        in_specs=[hbm, hbm, vmem, hbm],
+        in_specs=[hbm, hbm, hbm, hbm],
         out_specs=vmem,
         scratch_shapes=[
+            pltpu.VMEM((2, width), jnp.float32),
             pltpu.VMEM((per, depth), jnp.bfloat16),
             pltpu.VMEM((n, 2 * per, depth // 2), jnp.bfloat16),
             pltpu.VMEM((depth, width), jnp.bfloat16),
             pltpu.VMEM((2, depth, tcols), jnp.bfloat16),
             pltpu.VMEM((2, n, n * per, width), jnp.bfloat16),
             pltpu.VMEM((2, n * per, tcols), jnp.float32),
-            dma((3,)),
+            dma((4,)),
             dma((n,)), dma((nz,)), dma((nz,)), dma((2 * nz,)),
             dma((2, n)), dma((nz,)), dma((2 * nz,)), dma((2 * nz,)), dma((4 * nz,)),
         ],

time: 36.5 us -> 35.8 us (0.981)
  Pallas kernels: 35 us -> 34.3 us
    pallas_call x1, Pallas kernels: 35 us -> 34.3 us  [per_device(): pl.pallas_call(functools.partial(kernel, nz), out_shape=jax.ShapeDtypeStr...]
where the time goes in v2:
time: 35.8 us; the launch traced here: 35.6 us
  Pallas kernels  34.3 us (96%)
  local copies, waits for them, and re-layouts  1.3 us (4%)
    pallas_call x1, Pallas kernels, per_device(): pl.pallas_call(functools.partial(kernel, nz), out_shape=jax.ShapeDtypeStr...  34.3 us
    unnamed x1, local copies, waits for them, and re-layouts  1.3 us

profile of v2, /device:TPU:0, one launch (start us, length us, event | category | flops | bytes accessed | tf_op | source)
XLA Modules:
  0.0 35.6 jit_solution(10546159977905311318)
XLA Ops:
  0.0 34.3 %shard_map.46 = f32[16,16]{1,0:T(8,128)} custom-call(bf16[2,8,4096]{2,1,0:T(8,128)(2,1)} %bitcast.4, bf16[1,2,4096,256]{3,2,1,0:T(8,128)(2,1)} %basis_hbm.1, f32[2,256]{1,0:T(2,128)} %bitcast.5, bf16[1,2,4096,512]{3,2,1,0:T(8,128)(2,1)} %train_hbm.1), custom_call_target="tpu_custom_call" | custom-call | tf_op jit(solution)/shard_map/pallas_call | solution.py:196
  34.3 1.3 %copy.6 = f32[16,16]{1,0:T(8,128)} copy(f32[16,16]{1,0:T(8,128)} %shard_map.46) | data formatting | bytes 2048
